TPU v7x, 32 devices: a whole 2x2x4 slice. The times are simulated.
32 devices in a mesh: grp: 4 (over z), fsdp: 2 (over core), tp: 4 (over y, x).
Axes of the slice: x: 2, y: 2, z: 4, core: 2. Of those that a mesh axis runs over, the one named last changes fastest.
Arguments:
- queries: bfloat16 [16, 8192], P('fsdp', 'tp'), may hold values from -96 to 96
- cache: bfloat16 [2, 16, 2048, 1024], P(None, 'fsdp', 'grp', 'tp'), may hold values from -4 to 4, as said below
- lengths: int32 [16], P('fsdp'), may hold values from 2 to 2048, as said below
- output_weight: bfloat16 [8192, 8192], P('tp'), may hold values from -0.5 to 0.5
- adapter_down_weight: bfloat16 [8192, 128], P('tp'), may hold values from -0.5 to 0.5
- adapter_up_weight: bfloat16 [128, 8192], P('fsdp', 'tp'), may hold values from -0.5 to 0.5
Outputs:
- projected: bfloat16 [16, 8192], P('fsdp', 'tp')
Inputs may be any that keep to these rules, and one draw needn't show every extreme that they name: `lengths`: every row has at least two live positions, and some row has all 2048. `cache`: slot s holds the same keys and values as every slot s2 with s2 * 1 == s * 1.
All inputs are finite; a program needn't handle non-finite values.
Results may differ from a plain program's by a relative error of at most 0.015.
Values may be sent and summed in bfloat16 or wider, within the bound.
A program may use at most 128 MiB of HBM per device.

v0:
```python
import jax
import jax.numpy as jnp
from jax import lax
from jax.sharding import PartitionSpec as P

HEAD_SIZE = 128


adapter_scale = 0.5
mask_fill = -1e30


def merged(value, axis, join):
    pieces = jax.tree.map(lambda part: lax.all_gather(part, axis), value)
    head = jax.tree.map(lambda part: part[0], pieces)
    tail = jax.tree.map(lambda part: part[1:], pieces)
    running, _ = lax.scan(lambda running, share: (join(running, share), None), head, tail)
    return running


def join_partial(first_part, second_part):
    best_one, total_one, sum_one = first_part
    best_two, total_two, sum_two = second_part
    best = jnp.maximum(best_one, best_two)
    scale_one = jnp.exp(best_one - best)
    scale_two = jnp.exp(best_two - best)
    totals = total_one * scale_one + total_two * scale_two
    weighted = sum_one * scale_one[..., None] + sum_two * scale_two[..., None]
    return (best, totals, weighted)


def per_device(queries, cache, lengths, output_weight, adapter_down_weight, adapter_up_weight):
    row_count, width_here = queries.shape
    ctx_here = cache.shape[2]
    heads_here = width_here // HEAD_SIZE
    slots_here = cache.shape[3] // HEAD_SIZE
    per_slot = heads_here // slots_here
    query_part = queries.reshape(row_count, slots_here, per_slot, HEAD_SIZE)
    key_part = cache[0].reshape(row_count, ctx_here, slots_here, HEAD_SIZE)
    value_part = cache[1].reshape(row_count, ctx_here, slots_here, HEAD_SIZE)
    scores = jnp.einsum("rsqd,rpsd->rsqp", query_part, key_part, preferred_element_type=jnp.float32)
    scores = scores * HEAD_SIZE ** (-0.5)
    positions = lax.axis_index("grp") * ctx_here + jnp.arange(ctx_here, dtype=jnp.int32)
    visible = (positions[None, :] < lengths[:, None])[:, None, None, :]
    scores = jnp.where(visible, scores, mask_fill)
    best = jnp.max(scores, axis=-1)
    weights = jnp.where(visible, jnp.exp(scores - best[..., None]), 0.0)
    totals = jnp.sum(weights, axis=-1)
    weighted = jnp.einsum(
        "rsqp,rpsd->rsqd",
        weights.astype(jnp.bfloat16),
        value_part,
        preferred_element_type=jnp.float32,
    )
    best, totals, weighted = merged((best, totals, weighted), "grp", join_partial)
    attended_values = (
        (weighted / totals[..., None]).astype(jnp.bfloat16).reshape(row_count, width_here)
    )
    value_partial = jnp.dot(attended_values, output_weight, preferred_element_type=jnp.float32)
    adapter_output = jnp.dot(
        attended_values, adapter_down_weight, preferred_element_type=jnp.float32
    )
    adapter_rows = lax.all_gather(adapter_up_weight, "fsdp", axis=0, tiled=True)
    projected = lax.psum_scatter(
        value_partial.astype(jnp.bfloat16), "tp", scatter_dimension=1, tiled=True
    ).astype(jnp.float32)
    total_rank = lax.psum(adapter_output, "tp")
    projected = projected + adapter_scale * jnp.dot(
        total_rank, adapter_rows.astype(jnp.float32), precision=lax.Precision.HIGHEST
    )
    return projected.astype(jnp.bfloat16)


def solution(mesh):
    placed = (
        P("fsdp", "tp"),
        P(None, "fsdp", "grp", "tp"),
        P("fsdp"),
        P("tp", None),
        P("tp", None),
        P("fsdp", "tp"),
    )
    return jax.shard_map(
        per_device, mesh=mesh, in_specs=placed, out_specs=P("fsdp", "tp"), check_vma=False
    )
```

profile of v0, /device:TPU:0, one launch (start us, length us, event | category | flops | bytes accessed | tf_op | source)
XLA Modules:
  0.0 108.2 jit_solution(13940115888829980988)
XLA Ops:
  6.5 4.6 %fusion.23 = (bf16[1,8,512,256]{3,2,1,0:T(8,128)(2,1)}, bf16[1,8,512,256]{3,2,1,0:T(8,128)(2,1)}) fusion(bf16[2,8,512,256]{3,2,1,0:T(8,128)(2,1)} %param.9), kind=kLoop, calls=%fused_computation.35 | loop fusion | bytes 8388608 | tf_op jit(solution)/shard_map/slice | solution.py:40
  11.1 2.9 %copy.61 = bf16[1,8,512,256]{2,3,1,0:T(8,128)(2,1)S(1)} copy(bf16[1,8,512,256]{3,2,1,0:T(8,128)(2,1)} %get-tuple-element.87) | data formatting | bytes 4194304
  14.1 0.1 broadcast_compare_fusion
  14.1 0.5 fusion.24
  14.6 14.8 %all-gather = f32[32,2,8]{2,1,0:T(2,128)S(1)} all-gather(f32[8,2,8]{2,1,0:T(2,128)S(1)} %get-tuple-element.88), channel_id=2, replica_groups=mesh['grp'=4,'fsdp'=2,'tp'=4] {'grp'}, dimensions={0}, use_global_device_ids=true | all-gather | bytes 2560 | tf_op jit(solution)/shard_map/all_gather | solution.py:14
  29.4 0.2 fusion.8
  29.6 13.2 %all-gather.1 = f32[32,2,8]{2,1,0:T(2,128)S(1)} all-gather(f32[8,2,8]{2,1,0:T(2,128)S(1)} %fusion.8), channel_id=3, replica_groups=mesh['grp'=4,'fsdp'=2,'tp'=4] {'grp'}, dimensions={0}, use_global_device_ids=true | all-gather | bytes 2560 | tf_op jit(solution)/shard_map/all_gather | solution.py:14
  42.8 2.9 %copy.62 = bf16[1,8,512,256]{2,3,1,0:T(8,128)(2,1)S(1)} copy(bf16[1,8,512,256]{3,2,1,0:T(8,128)(2,1)} %get-tuple-element.86) | data formatting | bytes 4194304
  45.7 0.0 slice-start
  45.7 0.0 slice-start.1
  45.7 0.7 fusion.9
  46.4 13.9 %all-gather.2 = f32[32,2,8,128]{3,2,1,0:T(8,128)S(1)} all-gather(f32[8,2,8,128]{3,2,1,0:T(8,128)S(1)} %fusion.9), channel_id=4, replica_groups=mesh['grp'=4,'fsdp'=2,'tp'=4] {'grp'}, dimensions={0}, use_global_device_ids=true | all-gather | bytes 327680 | tf_op jit(solution)/shard_map/all_gather | solution.py:14
  60.4 0.6 while.14
  60.5 0.1 fusion.34
  60.7 0.1 fusion.34
  60.9 0.1 fusion.34
  61.0 0.1 fusion.18
  61.1 13.5 %convolution_convert_fusion = bf16[8,8192]{1,0:T(8,128)(2,1)} fusion(bf16[2048,8192]{1,0:T(8,128)(2,1)} %param.11, bf16[1,8,16,128]{3,2,1,0:T(8,128)(2,1)S(1)} %fusion.18), kind=kOutput, calls=%fused_computation.11 | convolution fusion | flops 268500992 | bytes 33718272 | tf_op jit(solution)/shard_map/dot_general | solution.py:59
  74.7 0.0 reduce-scatter.2.cloned.1.call-update
  74.7 0.2 fusion.14
  74.9 9.9 %psum.7 = f32[8,128]{1,0:T(8,128)S(1)} all-reduce(f32[8,128]{1,0:T(8,128)S(1)} %fusion.14), channel_id=1, replica_groups=mesh['grp'=4,'fsdp'=2,'tp'=4] {'tp'}, use_global_device_ids=true, to_apply=%region_5.6 | all-reduce | flops 1024 | bytes 8192 | tf_op jit(solution)/shard_map/psum | solution.py:67
  84.8 2.2 %all_gather.27 = bf16[128,2048]{1,0:T(8,128)(2,1)S(1)} all-gather(bf16[64,2048]{1,0:T(8,128)(2,1)S(1)} %copy-done.1), channel_id=1, replica_groups=mesh['grp'=4,'fsdp'=2,'tp'=4] {'fsdp'}, dimensions={0}, use_global_device_ids=true | all-gather | bytes 786432 | tf_op jit(solution)/shard_map/all_gather | solution.py:63
  86.9 12.7 %reduce-scatter.2.cloned.1.call-done = bf16[8,2048]{1,0:T(8,128)(2,1)} async-done(((bf16[8,8192]{1,0:T(8,128)(2,1)}), bf16[8,2048]{1,0:T(8,128)(2,1)}) %reduce-scatter.2.cloned.1.call-update) | async-done | bytes 32784 | tf_op jit(solution)/shard_map/reduce_scatter | solution.py:64
  99.7 1.7 %fusion.5 = bf16[8,2048]{1,0:T(8,128)(2,1)} fusion(f32[8,128]{1,0:T(8,128)S(1)} %psum.7, bf16[128,2048]{1,0:T(8,128)(2,1)S(1)} %all_gather.27, bf16[8,2048]{1,0:T(8,128)(2,1)} %reduce-scatter.2.cloned.1.call-done), kind=kOutput, calls=%fused_computation.14 | convolution fusion | flops 25231360 | bytes 593920 | tf_op jit(solution)/shard_map/dot_general | solution.py:68
  (37 shorter events, 0.2 us)
Async XLA Ops:
  6.5 68.1 %copy-start = (bf16[2048,128]{1,0:T(8,128)(2,1)S(1)}, bf16[2048,128]{1,0:T(8,128)(2,1)}, u32[]{:S(2)}) copy-start(bf16[2048,128]{1,0:T(8,128)(2,1)} %param.12) | copy-start | bytes 1572868
  6.5 93.1 %reduce-scatter.2.cloned.1.call-start = ((), (), s32[]{:S(2)}) async-start(), calls=%async_computation.1 | async-start | bytes 163840 | tf_op jit(solution)/shard_map/reduce_scatter | solution.py:64
  11.1 2.9 %copy-start.5 = (s32[8]{0:T(128)S(1)}, s32[8]{0:T(128)}, u32[]{:S(2)}) copy-start(s32[8]{0:T(128)} %param.10) | copy-start | bytes 100
  11.1 3.0 %copy-start.4 = (bf16[8,2048]{1,0:T(8,128)(2,1)S(1)}, bf16[8,2048]{1,0:T(8,128)(2,1)}, u32[]{:S(2)}) copy-start(bf16[8,2048]{1,0:T(8,128)(2,1)} %param.8) | copy-start | bytes 98308
  29.4 16.2 %copy-start.2 = (f32[32,2,8]{2,1,0:T(2,128)}, f32[32,2,8]{2,1,0:T(2,128)S(1)}, u32[]{:S(2)}) copy-start(f32[32,2,8]{2,1,0:T(2,128)S(1)} %all-gather) | copy-start | bytes 6148
  42.8 2.9 %copy-start.3 = (f32[32,2,8]{2,1,0:T(2,128)}, f32[32,2,8]{2,1,0:T(2,128)S(1)}, u32[]{:S(2)}) copy-start(f32[32,2,8]{2,1,0:T(2,128)S(1)} %all-gather.1) | copy-start | bytes 6148
  45.7 14.7 %slice-start = ((f32[32,2,8]{2,1,0:T(2,128)}), f32[8,2,8]{2,1,0:T(2,128)S(1)}, s32[]{:S(2)}) async-start(f32[32,2,8]{2,1,0:T(2,128)} %copy-done.2), calls=%async_computation.2 | async-start | bytes 16384 | tf_op jit(solution)/shard_map/slice | solution.py:15
  45.7 14.7 %slice-start.2 = ((f32[32,2,8]{2,1,0:T(2,128)}), f32[8,2,8]{2,1,0:T(2,128)S(1)}, s32[]{:S(2)}) async-start(f32[32,2,8]{2,1,0:T(2,128)} %copy-done.3), calls=%async_computation.4 | async-start | bytes 16384 | tf_op jit(solution)/shard_map/slice | solution.py:15
  45.7 14.7 %slice-start.1 = ((f32[32,2,8]{2,1,0:T(2,128)}), f32[24,2,8]{2,1,0:T(2,128)S(1)}, s32[]{:S(2)}) async-start(f32[32,2,8]{2,1,0:T(2,128)} %copy-done.2), calls=%async_computation.3 | async-start | bytes 49152 | tf_op jit(solution)/shard_map/slice | solution.py:16
  45.7 14.7 %slice-start.3 = ((f32[32,2,8]{2,1,0:T(2,128)}), f32[24,2,8]{2,1,0:T(2,128)S(1)}, s32[]{:S(2)}) async-start(f32[32,2,8]{2,1,0:T(2,128)} %copy-done.3), calls=%async_computation.5 | async-start | bytes 49152 | tf_op jit(solution)/shard_map/slice | solution.py:16
  61.1 23.7 %copy-start.1 = (bf16[64,2048]{1,0:T(8,128)(2,1)S(1)}, bf16[64,2048]{1,0:T(8,128)(2,1)}, u32[]{:S(2)}) copy-start(bf16[64,2048]{1,0:T(8,128)(2,1)} %param.13) | copy-start | bytes 786436
Sparse Core Ops, SparseCore 0:
  74.8 24.8 reduce-scatter.1
where the time goes:
time: 109 us; the launch traced here: 108 us
  blocking collectives  53.9 us (49%)
  matrix products  16.6 us (15%)
  between operations  13.6 us (12%)
  waiting for transfers between devices  12.7 us (12%)
  local copies, waits for them, and re-layouts  10.5 us (10%)
    all_gather x3, blocking collectives, merged(): pieces = jax.tree.map(lambda part: lax.all_gather(part, axis), value)  41.9 us
    dot_general x1, matrix products, per_device(): jnp.dot(attended_values, output_weight, preferred_element_type=jnp.float32)  13.5 us
    reduce_scatter x1, waiting for transfers between devices, per_device(): lax.psum_scatter(value_partial.astype(jnp.bfloat16), 'tp', scatter_dimens...  12.7 us
    psum x1, blocking collectives, per_device(): total_rank = lax.psum(adapter_output, 'tp')  9.9 us
    unnamed x14, local copies, waits for them, and re-layouts  5.78 us
    slice x1, local copies, waits for them, and re-layouts, per_device(): value_part = cache[1].reshape(row_count, ctx_here, slots_here, HEAD_SIZE)  4.6 us
  transfers between devices with their start and end apart: 1, of which 1 were waited for; matrix products, arithmetic and copies ran while one was open for 0% of the time, Pallas kernels for 0%

commit v1 on v0

v1 whole, which is shorter than its diff:
```python
import functools
import math

import jax
import jax.numpy as jnp
from jax import lax
from jax.experimental import pallas as pl
from jax.experimental.pallas import tpu as pltpu
from jax.sharding import PartitionSpec as P

HEAD_SIZE = 128
adapter_scale = 0.5
mask_fill = -1e30
LANES = 128
MESH = pl.DeviceIdType.MESH


def pack(value):
    c = value.shape[1]
    if c % (2 * LANES) == 0:
        both = jnp.concatenate([value[:, : c // 2], value[:, c // 2 :]], axis=0)
    else:
        both = jnp.concatenate([value, jnp.zeros_like(value)], axis=0)
    return both.astype(jnp.bfloat16)


def unpack(both, c):
    both = both.astype(jnp.float32)
    rows = both.shape[0] // 2
    if c % (2 * LANES) == 0:
        return jnp.concatenate([both[:rows], both[rows:]], axis=1)
    return both[:rows]


def kernel(
    sizes,
    lengths_ref,
    queries_hbm,
    cache_hbm,
    weight_hbm,
    down_hbm,
    up_hbm,
    out_ref,
    q_buf,
    q_heads,
    cache_buf,
    weight_buf,
    down_buf,
    up_buf,
    mine_u,
    mine_s,
    got_u,
    got_s,
    att,
    part_out,
    part_in,
    rank_out,
    rank_in,
    cols,
    q_sem,
    cache_sem,
    weight_sem,
    down_sem,
    up_sem,
    up_send,
    up_recv,
    u_send,
    u_recv,
    s_send,
    s_recv,
    part_send,
    part_recv,
    rank_send,
    rank_recv,
    cols_send,
    cols_recv,
):
    grp, fsdp, tp, rows, heads, slots, ctx, split, piece, groups, padded = sizes
    per_slot = heads // slots
    group_rows = rows // groups
    width = slots * HEAD_SIZE
    here = lax.axis_index("grp")
    side = lax.axis_index("fsdp")
    place = lax.axis_index("tp")
    part = lax.rem(here, split)

    barrier = pltpu.get_barrier_semaphore()
    for axis, size, at in (("grp", grp, here), ("fsdp", fsdp, side), ("tp", tp, place)):
        for step in range(1, size):
            pl.semaphore_signal(
                barrier, inc=1, device_id={axis: lax.rem(at + step, size)}, device_id_type=MESH
            )

    q_copy = pltpu.make_async_copy(queries_hbm, q_buf, q_sem)
    q_copy.start()
    cache_copies = []
    for n in range(groups):
        these = pl.ds(n * group_rows, group_rows)
        for kv in range(2):
            copy = pltpu.make_async_copy(
                cache_hbm.at[kv, these], cache_buf.at[kv, these], cache_sem.at[n, kv]
            )
            copy.start()
            cache_copies.append(copy)
    up_copy = pltpu.make_async_copy(
        up_hbm.at[:, pl.ds(pl.multiple_of(part * piece, LANES), piece)], up_buf.at[side], up_sem
    )
    up_copy.start()
    down_copy = pltpu.make_async_copy(down_hbm, down_buf, down_sem)
    down_copy.start()
    weight_copies = []
    for step in list(range(1, tp)) + [0]:
        target = lax.rem(place + step, tp)
        at = pl.multiple_of(target * (split * piece) + part * piece, LANES)
        copy = pltpu.make_async_copy(
            weight_hbm.at[:, pl.ds(at, piece)], weight_buf.at[step], weight_sem.at[step]
        )
        copy.start()
        weight_copies.append((step, copy))

    q_copy.wait()
    if padded != heads:
        q_heads[...] = jnp.zeros_like(q_heads)
    for h in range(heads):
        q_heads[:, h, :] = q_buf[:, h * HEAD_SIZE : (h + 1) * HEAD_SIZE].astype(jnp.float32)
    head_of = lax.broadcasted_iota(jnp.int32, (padded, HEAD_SIZE), 0)
    positions = here * ctx + lax.broadcasted_iota(jnp.int32, (padded, ctx), 1)
    lane = lax.broadcasted_iota(jnp.int32, (padded, LANES), 1)
    stats = jnp.full((padded, LANES), mask_fill, jnp.float32)
    for n in range(groups):
        cache_copies[2 * n].wait()
        each = range(n * group_rows, (n + 1) * group_rows)
        weights, totals = {}, {}
        for r in each:
            q = q_heads[r]
            blocks = [
                jnp.where((head_of >= s * per_slot) & (head_of < (s + 1) * per_slot), q, 0.0)
                for s in range(slots)
            ]
            spread = jnp.concatenate(blocks, axis=1).astype(jnp.bfloat16)
            scores = lax.dot_general(
                spread,
                cache_buf[0, r],
                (((1,), (1,)), ((), ())),
                preferred_element_type=jnp.float32,
            )
            scores = scores * HEAD_SIZE ** (-0.5)
            visible = positions < lengths_ref[r]
            scores = jnp.where(visible, scores, mask_fill)
            best = jnp.max(scores, axis=1, keepdims=True)
            weight = jnp.where(visible, jnp.exp(scores - best), 0.0)
            total = jnp.sum(weight, axis=1, keepdims=True)
            total = jnp.maximum(total, 1.0)
            stats = jnp.where(lane == r, best + jnp.log(total), stats)
            weights[r] = weight.astype(jnp.bfloat16)
            totals[r] = total
        cache_copies[2 * n + 1].wait()
        for r in each:
            summed = jnp.dot(weights[r], cache_buf[1, r], preferred_element_type=jnp.float32)
            mixed = summed[:, :HEAD_SIZE]
            for s in range(1, slots):
                mixed = jnp.where(
                    head_of >= s * per_slot, summed[:, s * HEAD_SIZE : (s + 1) * HEAD_SIZE], mixed
                )
            mine_u[r * padded : (r + 1) * padded] = (mixed / totals[r]).astype(jnp.bfloat16)
    mine_s[...] = stats

    up_copy.wait()
    pl.semaphore_wait(barrier, grp + fsdp + tp - 3)

    def send(src, dst, send_sem, recv_sem, target):
        copy = pltpu.make_async_remote_copy(
            src_ref=src,
            dst_ref=dst,
            send_sem=send_sem,
            recv_sem=recv_sem,
            device_id=target,
            device_id_type=MESH,
        )
        copy.start()
        return copy

    merges = []
    for step in range(1, grp):
        target = {"grp": lax.rem(here + step, grp)}
        k = step - 1
        merges.append(send(mine_s, got_s.at[k], s_send.at[k], s_recv.at[k], target))
        merges.append(send(mine_u, got_u.at[k], u_send.at[k], u_recv.at[k], target))
    ups = []
    for step in range(1, fsdp):
        target = {"fsdp": lax.rem(side + step, fsdp)}
        k = step - 1
        ups.append(send(up_buf.at[side], up_buf.at[side], up_send.at[k], up_recv.at[k], target))

    for k in range(grp - 1):
        merges[2 * k].wait_recv()
    shares = [mine_s[...]] + [got_s[k] for k in range(grp - 1)]
    top = functools.reduce(jnp.maximum, shares)
    shares = [jnp.exp(share - top) for share in shares]
    whole = functools.reduce(jnp.add, shares)
    shares = [share / whole for share in shares]
    for k in range(grp - 1):
        merges[2 * k + 1].wait_recv()
    for r in range(rows):
        these = slice(r * padded, (r + 1) * padded)
        value = mine_u[these].astype(jnp.float32) * shares[0][:, r : r + 1]
        for k in range(grp - 1):
            value = value + got_u[k, these].astype(jnp.float32) * shares[k + 1][:, r : r + 1]
        att[r] = value
    x = jnp.concatenate([att[:, h, :] for h in range(heads)], axis=1).astype(jnp.bfloat16)

    down_copy.wait()
    rank = jnp.dot(x, down_buf[...], preferred_element_type=jnp.float32)
    rank_out[...] = rank
    ranks = []
    for step in range(1, tp):
        target = {"tp": lax.rem(place + step, tp)}
        k = step - 1
        ranks.append(send(rank_out, rank_in.at[k], rank_send.at[k], rank_recv.at[k], target))
    parts = []
    own = None
    for step, copy in weight_copies:
        copy.wait()
        product = jnp.dot(x, weight_buf[step], preferred_element_type=jnp.float32)
        if step == 0:
            own = product
        else:
            k = step - 1
            target = {"tp": lax.rem(place + step, tp)}
            part_out[k] = pack(product)
            parts.append(
                send(part_out.at[k], part_in.at[k], part_send.at[k], part_recv.at[k], target)
            )

    for copy in ups:
        copy.wait_recv()
    for k in range(tp - 1):
        ranks[k].wait_recv()
        rank = rank + rank_in[k]
    high = rank.astype(jnp.bfloat16).astype(jnp.float32)
    middle = (rank - high).astype(jnp.bfloat16).astype(jnp.float32)
    low = rank - high - middle
    pieces = jnp.concatenate([high, middle, low], axis=0).astype(jnp.bfloat16)
    second = jnp.concatenate([up_buf[i] for i in range(fsdp)], axis=0)
    adapted = jnp.dot(pieces, second, preferred_element_type=jnp.float32)
    adapted = adapted[:rows] + adapted[rows : 2 * rows] + adapted[2 * rows :]
    result = own + adapter_scale * adapted
    for k in range(tp - 1):
        parts[k].wait_recv()
        result = result + unpack(part_in[k], piece)
    cols[part] = pack(result)

    gathers = []
    for step in range(1, split):
        target = {"grp": here - part + lax.rem(part + step, split)}
        k = step - 1
        gathers.append(
            send(cols.at[part], cols.at[part], cols_send.at[k], cols_recv.at[k], target)
        )
    for copy in merges + ups + ranks + parts:
        copy.wait_send()
    for step in range(1, split):
        source = lax.rem(part - step + split, split)
        k = step - 1
        pltpu.make_async_remote_copy(
            src_ref=cols.at[source],
            dst_ref=cols.at[source],
            send_sem=cols_send.at[k],
            recv_sem=cols_recv.at[k],
            device_id={"grp": here - part + source},
            device_id_type=MESH,
        ).wait_recv()
    for n in range(split):
        out_ref[:, n * piece : (n + 1) * piece] = unpack(cols[n], piece).astype(out_ref.dtype)
    for copy in gathers:
        copy.wait_send()


def per_device(sizes, queries, cache, lengths, weight, down, up):
    grp, fsdp, tp, rows, heads, slots, ctx, split, piece, groups, padded = sizes
    bf16, f32 = jnp.bfloat16, jnp.float32
    packed = (2 * rows, piece // 2 if piece % (2 * LANES) == 0 else piece)
    rank = down.shape[1]
    dma = pltpu.SemaphoreType.DMA
    some = lambda n: max(n, 1)
    return pl.pallas_call(
        functools.partial(kernel, sizes),
        out_shape=jax.ShapeDtypeStruct((rows, split * piece), bf16),
        in_specs=[pl.BlockSpec(memory_space=pltpu.SMEM)]
        + [pl.BlockSpec(memory_space=pltpu.HBM)] * 5,
        out_specs=pl.BlockSpec(memory_space=pltpu.VMEM),
        scratch_shapes=[
            pltpu.VMEM(queries.shape, bf16),
            pltpu.VMEM((rows, padded, HEAD_SIZE), f32),
            pltpu.VMEM(cache.shape, bf16),
            pltpu.VMEM((tp, weight.shape[0], piece), bf16),
            pltpu.VMEM(down.shape, bf16),
            pltpu.VMEM((fsdp, up.shape[0], piece), bf16),
            pltpu.VMEM((rows * padded, HEAD_SIZE), bf16),
            pltpu.VMEM((padded, LANES), f32),
            pltpu.VMEM((some(grp - 1), rows * padded, HEAD_SIZE), bf16),
            pltpu.VMEM((some(grp - 1), padded, LANES), f32),
            pltpu.VMEM((rows, padded, HEAD_SIZE), f32),
            pltpu.VMEM((some(tp - 1),) + packed, bf16),
            pltpu.VMEM((some(tp - 1),) + packed, bf16),
            pltpu.VMEM((rows, rank), f32),
            pltpu.VMEM((some(tp - 1), rows, rank), f32),
            pltpu.VMEM((split,) + packed, bf16),
            dma,
            dma((groups, 2)),
            dma((tp,)),
            dma,
            dma,
            dma((some(fsdp - 1),)),
            dma((some(fsdp - 1),)),
        ]
        + [dma((some(grp - 1),))] * 4
        + [dma((some(tp - 1),))] * 4
        + [dma((some(split - 1),))] * 2,
        compiler_params=pltpu.CompilerParams(
            collective_id=0, has_side_effects=True, vmem_limit_bytes=63 * 2**20
        ),
        name="decode_step",
    )(lengths, queries, cache, weight, down, up)


def solution(mesh):
    grp, fsdp, tp = (mesh.shape[axis] for axis in ("grp", "fsdp", "tp"))
    placed = (
        P("fsdp", "tp"),
        P(None, "fsdp", "grp", "tp"),
        P("fsdp"),
        P("tp", None),
        P("tp", None),
        P("fsdp", "tp"),
    )

    def local(queries, cache, lengths, weight, down, up):
        rows, width = queries.shape
        heads = width // HEAD_SIZE
        slots = cache.shape[3] // HEAD_SIZE
        columns = up.shape[1]
        split = math.gcd(grp, columns // LANES)
        groups = math.gcd(rows, 2)
        padded = -(-heads // 16) * 16
        sizes = (
            grp, fsdp, tp, rows, heads, slots, cache.shape[2], split, columns // split, groups, padded
        )
        return per_device(sizes, queries, cache, lengths, weight, down, up)

    return jax.shard_map(
        local, mesh=mesh, in_specs=placed, out_specs=P("fsdp", "tp"), check_vma=False
    )
```

time: 109 us -> 24.6 us (0.23)
  blocking collectives: 53.9 us -> 0 us
  Pallas kernels: 0 us -> 23 us
  matrix products: 16.6 us -> 0 us
  between operations: 13.6 us -> 0.01 us
  waiting for transfers between devices: 12.7 us -> 0 us
  local copies, waits for them, and re-layouts: 10.5 us -> 1.38 us
    all_gather x4 -> x0, blocking collectives: 44 us -> none  [the longest x3 41.9 us: merged(): pieces = jax.tree.map(lambda part: lax.all_gather(part, axis), value)]
    pallas_call x0 -> x1, Pallas kernels: none -> 23 us  [per_device(): pl.pallas_call(functools.partial(kernel, sizes), out_shape=jax.ShapeDtype...]
    dot_general x5 -> x0, matrix products: 16.6 us -> none  [the longest x1 13.5 us: per_device(): jnp.dot(attended_values, output_weight, preferred_element_type=jnp.float32)]
    reduce_scatter x1 -> x0, waiting for transfers between devices: 12.7 us -> none  [per_device(): lax.psum_scatter(value_partial.astype(jnp.bfloat16), 'tp', scatter_dimens...]
    psum x1 -> x0, blocking collectives: 9.9 us -> none  [per_device(): total_rank = lax.psum(adapter_output, 'tp')]
    slice x11 -> x0, local copies, waits for them, and re-layouts: 4.64 us -> none  [the longest x1 4.6 us: per_device(): value_part = cache[1].reshape(row_count, ctx_here, slots_here, HEAD_SIZE)]
    unnamed x14 -> x1, local copies, waits for them, and re-layouts: 5.78 us -> 1.38 us
  transfers between devices with their start and end apart: 1 -> 0, of which waited for: 1 -> 0; matrix products, arithmetic and copies ran while one was open for 0% -> 0% of each run, Pallas kernels for 0% -> 0%
where the time goes in v1:
time: 24.6 us; the launch traced here: 24.4 us
  Pallas kernels  23 us (93%)
  local copies, waits for them, and re-layouts  1.38 us (6%)
    pallas_call x1, Pallas kernels, per_device(): pl.pallas_call(functools.partial(kernel, sizes), out_shape=jax.ShapeDtype...  23 us
    unnamed x1, local copies, waits for them, and re-layouts  1.38 us

profile of v1, /device:TPU:0, one launch (start us, length us, event | category | flops | bytes accessed | tf_op | source)
XLA Modules:
  0.0 24.4 jit_solution(15171505091650568363)
XLA Ops:
  0.0 23.0 %decode_step.1 = bf16[8,2048]{1,0:T(8,128)(2,1)} custom-call(s32[8]{0:T(128)} %lengths_ref.1, bf16[8,2048]{1,0:T(8,128)(2,1)} %queries_hbm.1, bf16[2,8,512,256]{3,2,1,0:T(8,128)(2,1)} %cache_hbm.1, bf16[2048,8192]{1,0:T(8,128)(2,1)} %weight_hbm.1, bf16[2048,128]{1,0:T(8,128)(2,1)} %down_hbm.1, bf16[64,2048]{1,0:T(8,128)(2,1)} %up_hbm.1), custom_call_target="tpu_custom_call" | custom-call | tf_op jit(solution)/shard_map/decode_step/pallas_call | solution.py:286
  23.0 1.4 %copy.8 = bf16[8,2048]{1,0:T(8,128)(2,1)} copy(bf16[8,2048]{1,0:T(8,128)(2,1)} %decode_step.1) | data formatting | bytes 65536

commit v2 on v1

--- a/solution.py
+++ b/solution.py
@@ -108,16 +108,6 @@
     up_copy.start()
     down_copy = pltpu.make_async_copy(down_hbm, down_buf, down_sem)
     down_copy.start()
-    weight_copies = []
-    for step in list(range(1, tp)) + [0]:
-        target = lax.rem(place + step, tp)
-        at = pl.multiple_of(target * (split * piece) + part * piece, LANES)
-        copy = pltpu.make_async_copy(
-            weight_hbm.at[:, pl.ds(at, piece)], weight_buf.at[step], weight_sem.at[step]
-        )
-        copy.start()
-        weight_copies.append((step, copy))
-
     q_copy.wait()
     if padded != heads:
         q_heads[...] = jnp.zeros_like(q_heads)
@@ -155,6 +145,16 @@
             weights[r] = weight.astype(jnp.bfloat16)
             totals[r] = total
         cache_copies[2 * n + 1].wait()
+        if n == groups - 1:
+            weight_copies = []
+            for step in list(range(1, tp)) + [0]:
+                target = lax.rem(place + step, tp)
+                at = pl.multiple_of(target * (split * piece) + part * piece, LANES)
+                copy = pltpu.make_async_copy(
+                    weight_hbm.at[:, pl.ds(at, piece)], weight_buf.at[step], weight_sem.at[step]
+                )
+                copy.start()
+                weight_copies.append((step, copy))
         for r in each:
             summed = jnp.dot(weights[r], cache_buf[1, r], preferred_element_type=jnp.float32)
             mixed = summed[:, :HEAD_SIZE]
@@ -341,7 +341,7 @@
         slots = cache.shape[3] // HEAD_SIZE
         columns = up.shape[1]
         split = math.gcd(grp, columns // LANES)
-        groups = math.gcd(rows, 2)
+        groups = 1
         padded = -(-heads // 16) * 16
         sizes = (
             grp, fsdp, tp, rows, heads, slots, cache.shape[2], split, columns // split, groups, padded

time: 24.6 us -> 22.1 us (0.90)
  Pallas kernels: 23 us -> 20.6 us
    pallas_call x1, Pallas kernels: 23 us -> 20.6 us  [per_device(): pl.pallas_call(functools.partial(kernel, sizes), out_shape=jax.ShapeDtype...]
where the time goes in v2:
time: 22.1 us; the launch traced here: 22 us
  Pallas kernels  20.6 us (93%)
  local copies, waits for them, and re-layouts  1.38 us (6%)
    pallas_call x1, Pallas kernels, per_device(): pl.pallas_call(functools.partial(kernel, sizes), out_shape=jax.ShapeDtype...  20.6 us
    unnamed x1, local copies, waits for them, and re-layouts  1.38 us

profile of v2, /device:TPU:0, one launch (start us, length us, event | category | flops | bytes accessed | tf_op | source)
XLA Modules:
  0.0 22.0 jit_solution(17951830529098508705)
XLA Ops:
  0.0 20.6 %decode_step.1 = bf16[8,2048]{1,0:T(8,128)(2,1)} custom-call(s32[8]{0:T(128)} %lengths_ref.1, bf16[8,2048]{1,0:T(8,128)(2,1)} %queries_hbm.1, bf16[2,8,512,256]{3,2,1,0:T(8,128)(2,1)} %cache_hbm.1, bf16[2048,8192]{1,0:T(8,128)(2,1)} %weight_hbm.1, bf16[2048,128]{1,0:T(8,128)(2,1)} %down_hbm.1, bf16[64,2048]{1,0:T(8,128)(2,1)} %up_hbm.1), custom_call_target="tpu_custom_call" | custom-call | tf_op jit(solution)/shard_map/decode_step/pallas_call | solution.py:286
  20.6 1.4 %copy.8 = bf16[8,2048]{1,0:T(8,128)(2,1)} copy(bf16[8,2048]{1,0:T(8,128)(2,1)} %decode_step.1) | data formatting | bytes 65536

commit v3 on v2

--- a/solution.py
+++ b/solution.py
@@ -34,13 +34,15 @@
 
 def kernel(
     sizes,
-    lengths_ref,
+    lengths_hbm,
     queries_hbm,
     cache_hbm,
     weight_hbm,
     down_hbm,
     up_hbm,
     out_ref,
+    lengths_ref,
+    lengths_sem,
     q_buf,
     q_heads,
     cache_buf,
@@ -84,15 +86,10 @@
     place = lax.axis_index("tp")
     part = lax.rem(here, split)
 
-    barrier = pltpu.get_barrier_semaphore()
-    for axis, size, at in (("grp", grp, here), ("fsdp", fsdp, side), ("tp", tp, place)):
-        for step in range(1, size):
-            pl.semaphore_signal(
-                barrier, inc=1, device_id={axis: lax.rem(at + step, size)}, device_id_type=MESH
-            )
-
     q_copy = pltpu.make_async_copy(queries_hbm, q_buf, q_sem)
     q_copy.start()
+    lengths_copy = pltpu.make_async_copy(lengths_hbm, lengths_ref, lengths_sem)
+    lengths_copy.start()
     cache_copies = []
     for n in range(groups):
         these = pl.ds(n * group_rows, group_rows)
@@ -102,12 +99,20 @@
             )
             copy.start()
             cache_copies.append(copy)
+    barrier = pltpu.get_barrier_semaphore()
+    for axis, size, at in (("grp", grp, here), ("fsdp", fsdp, side), ("tp", tp, place)):
+        for step in range(1, size):
+            pl.semaphore_signal(
+                barrier, inc=1, device_id={axis: lax.rem(at + step, size)}, device_id_type=MESH
+            )
+
     up_copy = pltpu.make_async_copy(
         up_hbm.at[:, pl.ds(pl.multiple_of(part * piece, LANES), piece)], up_buf.at[side], up_sem
     )
     up_copy.start()
     down_copy = pltpu.make_async_copy(down_hbm, down_buf, down_sem)
     down_copy.start()
+    lengths_copy.wait()
     q_copy.wait()
     if padded != heads:
         q_heads[...] = jnp.zeros_like(q_heads)
@@ -286,10 +291,11 @@
     return pl.pallas_call(
         functools.partial(kernel, sizes),
         out_shape=jax.ShapeDtypeStruct((rows, split * piece), bf16),
-        in_specs=[pl.BlockSpec(memory_space=pltpu.SMEM)]
-        + [pl.BlockSpec(memory_space=pltpu.HBM)] * 5,
+        in_specs=[pl.BlockSpec(memory_space=pltpu.HBM)] * 6,
         out_specs=pl.BlockSpec(memory_space=pltpu.VMEM),
         scratch_shapes=[
+            pltpu.SMEM(lengths.shape, jnp.int32),
+            dma,
             pltpu.VMEM(queries.shape, bf16),
             pltpu.VMEM((rows, padded, HEAD_SIZE), f32),
             pltpu.VMEM(cache.shape, bf16),
@@ -340,7 +346,7 @@
         heads = width // HEAD_SIZE
         slots = cache.shape[3] // HEAD_SIZE
         columns = up.shape[1]
-        split = math.gcd(grp, columns // LANES)
+        split = 1
         groups = 1
         padded = -(-heads // 16) * 16
         sizes = (

time: 22.1 us -> 20.1 us (0.910)
  Pallas kernels: 20.6 us -> 18.6 us
    pallas_call x1, Pallas kernels: 20.6 us -> 18.6 us  [per_device(): pl.pallas_call(functools.partial(kernel, sizes), out_shape=jax.ShapeDtype...]
where the time goes in v3:
time: 20.1 us; the launch traced here: 20 us
  Pallas kernels  18.6 us (93%)
  local copies, waits for them, and re-layouts  1.38 us (7%)
    pallas_call x1, Pallas kernels, per_device(): pl.pallas_call(functools.partial(kernel, sizes), out_shape=jax.ShapeDtype...  18.6 us
    unnamed x1, local copies, waits for them, and re-layouts  1.38 us

profile of v3, /device:TPU:0, one launch (start us, length us, event | category | flops | bytes accessed | tf_op | source)
XLA Modules:
  0.0 20.0 jit_solution(2363950578651942231)
XLA Ops:
  0.0 18.6 %decode_step.1 = bf16[8,2048]{1,0:T(8,128)(2,1)} custom-call(s32[8]{0:T(128)} %lengths_hbm.1, bf16[8,2048]{1,0:T(8,128)(2,1)} %queries_hbm.1, bf16[2,8,512,256]{3,2,1,0:T(8,128)(2,1)} %cache_hbm.1, bf16[2048,8192]{1,0:T(8,128)(2,1)} %weight_hbm.1, bf16[2048,128]{1,0:T(8,128)(2,1)} %down_hbm.1, bf16[64,2048]{1,0:T(8,128)(2,1)} %up_hbm.1), custom_call_target="tpu_custom_call" | custom-call | tf_op jit(solution)/shard_map/decode_step/pallas_call | solution.py:291
  18.6 1.4 %copy.8 = bf16[8,2048]{1,0:T(8,128)(2,1)} copy(bf16[8,2048]{1,0:T(8,128)(2,1)} %decode_step.1) | data formatting | bytes 65536
